TPU v7x, 32 devices: a whole 2x2x4 slice. The times are simulated.
32 devices in a mesh: seq: 16 (over z, y, x), head: 2 (over core).
Axes of the slice: x: 2, y: 2, z: 4, core: 2. Of those that a mesh axis runs over, the one named last changes fastest.
Arguments:
- activations: bfloat16 [8192, 2048], P('seq', 'head'), may hold values from -6 to 6
- w_proj: bfloat16 [3, 2048, 2048], P(None, None, 'head'), may hold values from -0.125 to 0.125
- level_weight: float32 [8192, 16, 14], P('seq', 'head'), may hold values from 0.25 to 4
- grad_out: bfloat16 [8192, 2048], P('seq', 'head'), may hold values from -6 to 6
Outputs:
- attn_output: bfloat16 [8192, 2048], P('seq', 'head')
- grad_query: bfloat16 [8192, 2048], P('seq', 'head')
- grad_key: bfloat16 [8192, 2048], P('seq', 'head')
- grad_value: bfloat16 [8192, 2048], P('seq', 'head')
All inputs are finite; a program needn't handle non-finite values.
Results may differ from a plain program's by a relative error of at most 0.0085.
Values may be sent and summed in bfloat16 or wider, within the bound.
A program may use at most 64 MiB of HBM per device.

v0:
```python
import functools

import jax
import jax.numpy as jnp
from jax import lax
from jax.experimental import pallas as pl
from jax.experimental.pallas import tpu as pltpu
from jax.sharding import PartitionSpec as P

MESH = pl.DeviceIdType.MESH
F32 = jnp.float32
BF16 = jnp.bfloat16


def dot_nn(a, b):
    return lax.dot_general(a, b, (((1,), (0,)), ((), ())), preferred_element_type=F32)


def dot_nt(a, b):
    return lax.dot_general(a, b, (((1,), (1,)), ((), ())), preferred_element_type=F32)


def dot_tn(a, b):
    return lax.dot_general(a, b, (((0,), (0,)), ((), ())), preferred_element_type=F32)


def level_factor(level):
    return 2.0 ** (-0.5 * (max(level, 1) - 1))


def diagonal_mask(rows, start, size, leaf, leaf_level):
    if size == leaf:
        total = jnp.zeros((leaf, leaf), F32)
        for level in range(leaf.bit_length()):
            row = rows[level : level + 1, start : start + leaf]
            total = jnp.where(leaf_level == level, row, total)
        return total
    half = size // 2
    early = diagonal_mask(rows, start, half, leaf, leaf_level)
    late = diagonal_mask(rows, start + half, half, leaf, leaf_level)
    level = half.bit_length()
    side = jnp.broadcast_to(
        rows[level : level + 1, start + half : start + size], (half, half)
    )
    return jnp.concatenate(
        [
            jnp.concatenate([early, side], 1),
            jnp.concatenate([jnp.zeros((half, half), F32), late], 1),
        ],
        0,
    )


def state_kernel(
    dims,
    act_ref,
    w_ref,
    lw_ref,
    cot_ref,
    out_ref,
    dq_ref,
    dk_ref,
    dv_ref,
    acts,
    w_vm,
    cot,
    partial,
    rows_vm,
    qkv,
    cots,
    qt_vm,
    kt_vm,
    vt_vm,
    ct_vm,
    group,
    rgrad,
    moving,
    s_send,
    s_recv,
    r_send,
    r_recv,
    upper,
    inner_t,
    inner,
    finals,
    act_sem,
    cot_sem,
    w_sem,
    act_send_sem,
    act_recv_sem,
    s_send_sem,
    s_recv_sem,
    r_send_sem,
    r_recv_sem,
    final_sem,
):
    n_seq, n_head, heads, head_dim, block, features, per = dims
    chunks = heads // per
    bits = n_seq.bit_length() - 1
    block_bits = block.bit_length() - 1
    scale = head_dim**-0.5
    width = per * head_dim
    seq = lax.axis_index("seq")
    head = lax.axis_index("head")
    bit_of = [lax.rem(seq // (1 << j), 2) for j in range(bits)]
    top = bits - 1
    below = bits - 2
    reach = 1 << below
    quarter = seq // reach
    partner_of = [seq + (1 << j) - 2 * (1 << j) * bit_of[j] for j in range(bits)]

    def weight_copy(c, chunk):
        return pltpu.make_async_copy(
            w_ref.at[c, :, pl.ds(pl.multiple_of(chunk * width, width), width)],
            w_vm.at[chunk, c],
            w_sem.at[c, chunk],
        )

    own = pltpu.make_async_copy(act_ref, acts.at[0], act_sem)
    own.start()
    weight_copy(1, 0).start()
    weight_copy(2, 0).start()
    cot_copy = pltpu.make_async_copy(cot_ref, cot, cot_sem)
    cot_copy.start()

    barrier = pltpu.get_barrier_semaphore()
    for r in range(1, n_head):
        pl.semaphore_signal(
            barrier, inc=1, device_id=(seq, lax.rem(head + r, n_head)), device_id_type=MESH
        )
    for j in range(top):
        pl.semaphore_signal(barrier, inc=1, device_id=(partner_of[j], head), device_id_type=MESH)

    @pl.when((quarter == 1) | (quarter == 2))
    def _():
        other = seq + reach * (3 - 2 * quarter)
        pl.semaphore_signal(barrier, inc=1, device_id=(other, head), device_id_type=MESH)

    peers = n_head - 1 + top
    middle_half = (quarter == 1) | (quarter == 2)
    pl.when(middle_half)(lambda: pl.semaphore_wait(barrier, peers + 1))
    pl.when(jnp.logical_not(middle_half))(lambda: pl.semaphore_wait(barrier, peers))

    def act_copy(r):
        return pltpu.make_async_remote_copy(
            src_ref=act_ref,
            dst_ref=acts.at[r],
            send_sem=act_send_sem.at[r],
            recv_sem=act_recv_sem.at[r],
            device_id=(seq, lax.rem(head + r, n_head)),
            device_id_type=MESH,
        )

    for r in range(1, n_head):
        act_copy(r).start()
    for chunk in range(1, chunks):
        weight_copy(1, chunk).start()
        weight_copy(2, chunk).start()
    for chunk in range(chunks):
        weight_copy(0, chunk).start()

    levels = lw_ref.shape[0]
    for h in range(heads):
        rows_vm[h] = jnp.concatenate(
            [lw_ref[level, h : h + 1, :] * (scale * level_factor(level)) for level in range(levels)]
            + [jnp.zeros((1, block), F32)] * (-levels % 8),
            0,
        )
    stages = bits + 1

    def s_way(stage):
        if stage < below:
            return None, None, partner_of[stage]
        if stage == below:
            return bit_of[below] == 0, bit_of[below] == 1, partner_of[below]
        return quarter == stage - below, quarter == stage - below + 1, None

    def r_way(stage):
        if stage < 2:
            return quarter == 3 - stage, quarter == 2 - stage, None
        bit = bits - stage
        if stage == 2:
            return bit_of[below] == 1, bit_of[below] == 0, partner_of[below]
        return None, None, partner_of[bit]

    def remote(send, recv, send_sem, recv_sem, stage, chunk, target):
        return pltpu.make_async_remote_copy(
            src_ref=send.at[stage, chunk],
            dst_ref=recv.at[stage, chunk],
            send_sem=send_sem.at[stage, chunk],
            recv_sem=recv_sem.at[stage, chunk],
            device_id=(target, head),
            device_id_type=MESH,
        )

    def s_copy(stage, chunk):
        target = s_way(stage)[2]
        target = seq + reach if target is None else target
        return remote(s_send, s_recv, s_send_sem, s_recv_sem, stage, chunk, target)

    def r_copy(stage, chunk):
        target = r_way(stage)[2]
        target = seq - reach if target is None else target
        return remote(r_send, r_recv, r_send_sem, r_recv_sem, stage, chunk, target)

    def only_if(condition, action):
        if condition is None:
            action()
        else:
            pl.when(condition)(action)

    def start_s(stage, chunk):
        def send():
            s_send[stage, chunk] = group[chunk].astype(BF16)
            s_copy(stage, chunk).start()

        only_if(s_way(stage)[0], send)

    def start_r(stage, chunk):
        bit = top if stage < 2 else bits - stage

        def send():
            term = rgrad[chunk, :, bit]
            if stage == 1:
                term = term + moving[chunk]
            if stage >= 2:
                term = moving[chunk] + bit_of[bit].astype(F32) * term
            r_send[stage, chunk] = term.astype(BF16)
            r_copy(stage, chunk).start()

        only_if(r_way(stage)[0], send)

    zero = (per, head_dim, head_dim)

    def finish_s(stage, chunk):
        def take():
            s_copy(stage, chunk).wait_recv()
            got = s_recv[stage, chunk]
            if stage < below:
                flag = bit_of[stage].astype(F32)
                upper[chunk, :, stage] = (got.astype(F32) * flag).astype(BF16)
            else:
                upper[chunk, :, min(stage, top)] = got
            if stage <= below:
                group[chunk] += got.astype(F32)
            if stage == top:
                group[chunk] = got.astype(F32)

        if stage == below:

            @pl.when(bit_of[below] == 0)
            def _():
                upper[chunk, :, below] = jnp.zeros(zero, BF16)

        if stage == top:

            @pl.when(quarter < 2)
            def _():
                upper[chunk, :, top] = jnp.zeros(zero, BF16)

        only_if(s_way(stage)[1], take)

    def finish_r(stage, chunk):
        def take():
            r_copy(stage, chunk).wait_recv()
            got = r_recv[stage, chunk].astype(F32)
            if stage < 2:
                moving[chunk] = got
            else:
                moving[chunk] += got

        if stage == 0:
            moving[chunk] = jnp.zeros(zero, F32)
        if stage == 2:

            @pl.when(quarter == 2)
            def _():
                moving[chunk] = jnp.zeros(zero, F32)

        only_if(r_way(stage)[1], take)

    lag = 2
    heads_end = 2 * chunks + heads
    s_base, r_base = chunks, chunks + lag
    last_slot = r_base + lag * bits + chunks - 1
    crossing_inside = all(
        r_base + lag * bits + c >= 2 * chunks + per * (c + 1) - 1 for c in range(chunks)
    )

    def tick(slot, low, high):
        for stage in range(stages):
            for base, finish, start, is_r in (
                (s_base, finish_s, start_s, False),
                (r_base, finish_r, start_r, True),
            ):
                first = base + lag * stage
                if first > high or first + chunks - 1 < low:
                    continue
                chunk = slot - first

                @pl.when((chunk >= 0) & (chunk < chunks))
                def _():
                    finish(stage, chunk)
                    if stage < bits:
                        start(stage + 1, chunk)
                    elif is_r and crossing_inside:
                        cross(chunk)

    def final_copies(chunk):
        lanes = pl.ds(pl.multiple_of(chunk * width, width), width)
        return [
            pltpu.make_async_copy(
                finals.at[n, :, lanes], target.at[:, lanes], final_sem.at[n, chunk]
            )
            for n, target in enumerate((out_ref, dq_ref, dk_ref, dv_ref))
        ]

    def cross(chunk):
        for i in range(per):
            h = chunk * per + i
            lanes = pl.ds(pl.multiple_of(h * head_dim, head_dim), head_dim)
            weights = rows_vm[h]

            def weighted(transposed):
                full = transposed.astype(F32)
                parts = []
                for j in range(bits):
                    level = block_bits + 1 + j
                    parts.append((full * weights[level : level + 1, :]).astype(BF16))
                return jnp.concatenate(parts, 0)

            states = upper[chunk, i]
            tall = states.reshape(bits * head_dim, head_dim)
            wide = jnp.concatenate([states[j] for j in range(bits)], 1)
            out_t = inner_t[0, h] + dot_nn(tall.T, weighted(qt_vm[h]))
            dq_t = inner_t[1, h] + dot_nn(wide, weighted(ct_vm[h]))
            finals[0, :, lanes] = out_t.astype(BF16).T
            finals[1, :, lanes] = dq_t.astype(BF16).T
            suffix = moving[chunk, i].astype(BF16)
            finals[2, :, lanes] = (inner[0, h] + dot_nt(qkv[2, h], suffix)).astype(BF16)
            finals[3, :, lanes] = (inner[1, h] + dot_nn(qkv[1, h], suffix)).astype(BF16)
        for copy in final_copies(chunk):
            copy.start()

    own.wait()
    offsets = [
        pl.multiple_of(lax.rem(head + n_head - r, n_head) * features, features)
        for r in range(n_head)
    ]

    def own_part(c, chunk):
        weight_copy(c, chunk).wait()
        partial[c] = dot_nn(acts[0], w_vm[chunk, c, pl.ds(offsets[0], features), :])

    def finish_projection(c, chunk):
        total = partial[c]
        for r in range(1, n_head):
            total += dot_nn(acts[r], w_vm[chunk, c, pl.ds(offsets[r], features), :])
        total = total.astype(BF16)
        for i in range(per):
            qkv[c, chunk * per + i] = total[:, i * head_dim : (i + 1) * head_dim]

    def project_kv(chunk, _):
        own_part(1, chunk)
        own_part(2, chunk)

        @pl.when(chunk == 0)
        def _():
            for r in range(1, n_head):
                act_copy(r).wait_recv()

        finish_projection(1, chunk)
        finish_projection(2, chunk)
        for i in range(per):
            h = chunk * per + i
            key_t = qkv[1, h].T
            group[chunk, i] = dot_nn(key_t, qkv[2, h])
            kt_vm[h] = key_t
            vt_vm[h] = qkv[2, h].T
        start_s(0, chunk)
        return 0

    lax.fori_loop(0, chunks, project_kv, 0)
    cot_copy.wait()

    def project_q(chunk, _):
        own_part(0, chunk)
        finish_projection(0, chunk)
        for i in range(per):
            h = chunk * per + i
            lanes = pl.ds(pl.multiple_of(h * head_dim, head_dim), head_dim)
            cotangent = cot[:, lanes]
            cots[h] = cotangent
            query_t = qkv[0, h].T
            wide = query_t.astype(F32)
            weights = rows_vm[h]
            for j in range(bits):
                level = block_bits + 1 + j
                weighted = (wide * weights[level : level + 1, :]).astype(BF16)
                rgrad[chunk, i, j] = dot_nn(weighted, cotangent)
            qt_vm[h] = query_t
            ct_vm[h] = cotangent.T
        start_r(0, chunk)
        tick(chunks + chunk, chunks, 2 * chunks - 1)
        return 0

    lax.fori_loop(0, chunks, project_q, 0)

    tile = min(2 * head_dim, block)
    leaf = min(head_dim, tile)
    tiles = block // tile
    early_ids = lax.broadcasted_iota(jnp.int32, (leaf, leaf), 0)
    late_ids = lax.broadcasted_iota(jnp.int32, (leaf, leaf), 1)
    differ = jnp.bitwise_xor(early_ids, late_ids)
    leaf_level = jnp.zeros((leaf, leaf), jnp.int32)
    for shift in range(leaf.bit_length() - 1):
        leaf_level = leaf_level + (differ >= (1 << shift)).astype(jnp.int32)
    leaf_level = jnp.where(early_ids <= late_ids, leaf_level, -1)

    def attend(h):
        weights = rows_vm[h]
        for a in range(tiles):
            here = slice(a * tile, (a + 1) * tile)
            end = (a + 1) * tile
            mask = []
            for b in range(a):
                level = tile.bit_length() - 1 + (a ^ b).bit_length()
                mask.append(jnp.broadcast_to(weights[level : level + 1, here], (tile, tile)))
            mask.append(diagonal_mask(weights, a * tile, tile, leaf, leaf_level))
            mask = jnp.concatenate(mask, 0) if a else mask[0]
            attn = (dot_nn(qkv[1, h, :end, :], qt_vm[h, :, here]) * mask).astype(BF16)
            grads = (dot_nn(qkv[2, h, :end, :], ct_vm[h, :, here]) * mask).astype(BF16)
            inner_t[0, h, :, here] = dot_nn(vt_vm[h, :, :end], attn)
            inner_t[1, h, :, here] = dot_nn(kt_vm[h, :, :end], grads)
            dk_part = dot_nn(grads, qkv[0, h, here, :])
            dv_part = dot_nn(attn, cots[h, here, :])
            if a:
                inner[0, h, : a * tile, :] += dk_part[: a * tile]
                inner[1, h, : a * tile, :] += dv_part[: a * tile]
            inner[0, h, here, :] = dk_part[a * tile :]
            inner[1, h, here, :] = dv_part[a * tile :]

    def middle(h, _):
        attend(h)
        tick(2 * chunks + h, 2 * chunks, heads_end - 1)
        return 0

    lax.fori_loop(0, heads, middle, 0)

    def settle(slot, _):
        tick(slot, heads_end, last_slot)
        return 0

    if last_slot >= heads_end:
        lax.fori_loop(heads_end, last_slot + 1, settle, 0)
    if not crossing_inside:

        def cross_one(chunk, _):
            cross(chunk)
            return 0

        lax.fori_loop(0, chunks, cross_one, 0)

    for r in range(1, n_head):
        act_copy(r).wait_send()

    def drain(chunk, _):
        for stage in range(stages):
            only_if(s_way(stage)[0], lambda: s_copy(stage, chunk).wait_send())
            only_if(r_way(stage)[0], lambda: r_copy(stage, chunk).wait_send())
        for copy in final_copies(chunk):
            copy.wait()
        return 0

    lax.fori_loop(0, chunks, drain, 0)


def hand_over_kernel(pieces, *refs):
    sources, targets, buffers = refs[:4], refs[4:8], refs[8]
    in_sem, out_sem = refs[9:]
    rows = sources[0].shape[0] // pieces
    order = [(n, piece) for piece in range(pieces) for n in range(4)]

    def copies(n, piece):
        part = pl.ds(piece * rows, rows)
        inward = pltpu.make_async_copy(
            sources[n].at[part], buffers.at[n, part], in_sem.at[n, piece]
        )
        outward = pltpu.make_async_copy(
            buffers.at[n, part], targets[n].at[part], out_sem.at[n, piece]
        )
        return inward, outward

    moves = [copies(n, piece) for n, piece in order]
    for inward, _ in moves:
        inward.start()
    for inward, outward in moves:
        inward.wait()
        outward.start()
    for _, outward in moves:
        outward.wait()


def on_device(n_seq, n_head, activations, w_proj, level_weight, grad_out):
    block, features = activations.shape
    width = w_proj.shape[2]
    heads = level_weight.shape[1]
    head_dim = width // heads
    per = 2 if heads % 2 == 0 else 1
    chunks = heads // per
    bits = n_seq.bit_length() - 1
    levels = level_weight.shape[2]
    padded = levels + (-levels % 8)
    dims = (n_seq, n_head, heads, head_dim, block, features, per)
    square = (head_dim, head_dim)
    tall = (block, head_dim)
    flat = (head_dim, block)
    dma = pltpu.SemaphoreType.DMA
    any_spec = pl.BlockSpec(memory_space=pl.ANY)
    vmem_spec = pl.BlockSpec(memory_space=pltpu.VMEM)
    results = [jax.ShapeDtypeStruct((block, width), BF16)] * 4
    parts = pl.pallas_call(
        functools.partial(state_kernel, dims),
        out_shape=results,
        in_specs=[any_spec, any_spec, vmem_spec, any_spec],
        out_specs=[any_spec] * 4,
        scratch_shapes=[
            pltpu.VMEM((n_head, block, features), BF16),
            pltpu.VMEM((chunks, 3, w_proj.shape[1], per * head_dim), BF16),
            pltpu.VMEM((block, width), BF16),
            pltpu.VMEM((3, block, per * head_dim), F32),
            pltpu.VMEM((heads, padded, block), F32),
            pltpu.VMEM((3, heads) + tall, BF16),
            pltpu.VMEM((heads,) + tall, BF16),
            pltpu.VMEM((heads,) + flat, BF16),
            pltpu.VMEM((heads,) + flat, BF16),
            pltpu.VMEM((heads,) + flat, BF16),
            pltpu.VMEM((heads,) + flat, BF16),
            pltpu.VMEM((chunks, per) + square, F32),
            pltpu.VMEM((chunks, per, bits) + square, F32),
            pltpu.VMEM((chunks, per) + square, F32),
            pltpu.VMEM((bits + 1, chunks, per) + square, BF16),
            pltpu.VMEM((bits + 1, chunks, per) + square, BF16),
            pltpu.VMEM((bits + 1, chunks, per) + square, BF16),
            pltpu.VMEM((bits + 1, chunks, per) + square, BF16),
            pltpu.VMEM((chunks, per, bits) + square, BF16),
            pltpu.VMEM((2, heads) + flat, F32),
            pltpu.VMEM((2, heads) + tall, F32),
            pltpu.VMEM((4, block, width), BF16),
            dma,
            dma,
            dma((3, chunks)),
            dma((n_head,)),
            dma((n_head,)),
            dma((bits + 1, chunks)),
            dma((bits + 1, chunks)),
            dma((bits + 1, chunks)),
            dma((bits + 1, chunks)),
            dma((4, chunks)),
        ],
        compiler_params=pltpu.CompilerParams(
            collective_id=0, has_side_effects=True, vmem_limit_bytes=56 * 2**20
        ),
    )(activations, w_proj, jnp.transpose(level_weight, (2, 1, 0)), grad_out)

    pieces = 2 if block % 256 == 0 else 1
    return pl.pallas_call(
        functools.partial(hand_over_kernel, pieces),
        out_shape=results,
        in_specs=[any_spec] * 4,
        out_specs=[any_spec] * 4,
        scratch_shapes=[
            pltpu.VMEM((4, block, width), BF16),
            dma((4, pieces)),
            dma((4, pieces)),
        ],
        compiler_params=pltpu.CompilerParams(vmem_limit_bytes=60 * 2**20),
    )(*parts)


def solution(mesh):
    in_specs = (P("seq", "head"), P(None, None, "head"), P("seq", "head", None), P("seq", "head"))
    out_specs = (P("seq", "head"), P("seq", "head"), P("seq", "head"), P("seq", "head"))
    return jax.shard_map(
        functools.partial(on_device, mesh.shape["seq"], mesh.shape["head"]),
        mesh=mesh,
        in_specs=in_specs,
        out_specs=out_specs,
        check_vma=False,
    )
```

profile of v0, /device:TPU:0, one launch (start us, length us, event | category | flops | bytes accessed | tf_op | source)
XLA Modules:
  0.0 47.5 jit_solution(7315069286604507640)
XLA Ops:
  0.6 43.3 %shard_map.75 = (bf16[512,1024]{1,0:T(8,128)(2,1)}, bf16[512,1024]{1,0:T(8,128)(2,1)}, bf16[512,1024]{1,0:T(8,128)(2,1)}, bf16[512,1024]{1,0:T(8,128)(2,1)}) custom-call(bf16[512,1024]{1,0:T(8,128)(2,1)} %act_ref.1, bf16[3,2048,1024]{2,1,0:T(8,128)(2,1)} %w_ref.1, f32[14,8,512]{2,1,0:T(8,128)} %bitcast.1, bf16[512,1024]{1,0:T(8,128)(2,1)} %cot_ref.1), custom_call_target="tpu_custom_call" | custom-call | tf_op jit(solution)/shard_map/pallas_call | solution.py:522
  44.0 3.6 %shard_map.76 = (bf16[512,1024]{1,0:T(8,128)(2,1)}, bf16[512,1024]{1,0:T(8,128)(2,1)}, bf16[512,1024]{1,0:T(8,128)(2,1)}, bf16[512,1024]{1,0:T(8,128)(2,1)}) custom-call(bf16[512,1024]{1,0:T(8,128)(2,1)} %get-tuple-element.8.refs_0_, bf16[512,1024]{1,0:T(8,128)(2,1)} %get-tuple-element.9.refs_1_, bf16[512,1024]{1,0:T(8,128)(2,1)} %get-tuple-element.10.refs_2_, ...), custom_call_target="tpu_custom_call" | custom-call | tf_op jit(solution)/shard_map/pallas_call | solution.py:567
where the time goes:
time: 47.7 us; the launch traced here: 47.5 us
  Pallas kernels  46.9 us (98%)
  between operations  0.64 us (1%)
    pallas_call x1, Pallas kernels, on_device(): pl.pallas_call(functools.partial(state_kernel, dims), out_shape=results,...  43.3 us
    pallas_call x1, Pallas kernels, on_device(): pl.pallas_call(functools.partial(hand_over_kernel, pieces), out_shape=res...  3.58 us

commit v1 on v0

--- a/solution.py
+++ b/solution.py
@@ -116,12 +116,12 @@
             w_sem.at[c, chunk],
         )
 
-    own = pltpu.make_async_copy(act_ref, acts.at[0], act_sem)
+    own_features = pl.ds(pl.multiple_of(head * features, features), features)
+    own = pltpu.make_async_copy(act_ref, acts.at[:, own_features], act_sem)
     own.start()
     weight_copy(1, 0).start()
     weight_copy(2, 0).start()
     cot_copy = pltpu.make_async_copy(cot_ref, cot, cot_sem)
-    cot_copy.start()
 
     barrier = pltpu.get_barrier_semaphore()
     for r in range(1, n_head):
@@ -144,7 +144,7 @@
     def act_copy(r):
         return pltpu.make_async_remote_copy(
             src_ref=act_ref,
-            dst_ref=acts.at[r],
+            dst_ref=acts.at[:, own_features],
             send_sem=act_send_sem.at[r],
             recv_sem=act_recv_sem.at[r],
             device_id=(seq, lax.rem(head + r, n_head)),
@@ -153,11 +153,6 @@
 
     for r in range(1, n_head):
         act_copy(r).start()
-    for chunk in range(1, chunks):
-        weight_copy(1, chunk).start()
-        weight_copy(2, chunk).start()
-    for chunk in range(chunks):
-        weight_copy(0, chunk).start()
 
     levels = lw_ref.shape[0]
     for h in range(heads):
@@ -343,34 +338,40 @@
             copy.start()
 
     own.wait()
-    offsets = [
-        pl.multiple_of(lax.rem(head + n_head - r, n_head) * features, features)
-        for r in range(n_head)
-    ]
-
-    def own_part(c, chunk):
-        weight_copy(c, chunk).wait()
-        partial[c] = dot_nn(acts[0], w_vm[chunk, c, pl.ds(offsets[0], features), :])
-
-    def finish_projection(c, chunk):
-        total = partial[c]
-        for r in range(1, n_head):
-            total += dot_nn(acts[r], w_vm[chunk, c, pl.ds(offsets[r], features), :])
+    def keep(c, chunk, total):
         total = total.astype(BF16)
         for i in range(per):
             qkv[c, chunk * per + i] = total[:, i * head_dim : (i + 1) * head_dim]
 
+    def project(c, chunk):
+        keep(c, chunk, dot_nn(acts[...], w_vm[chunk, c]))
+
     def project_kv(chunk, _):
-        own_part(1, chunk)
-        own_part(2, chunk)
+        for c in (1, 2):
+            pl.when(chunk + 1 < chunks)(lambda: weight_copy(c, chunk + 1).start())
+            weight_copy(c, chunk).wait()
 
         @pl.when(chunk == 0)
         def _():
+            for c in (1, 2):
+                partial[c - 1] = dot_nn(acts[:, own_features], w_vm[0, c, own_features, :])
+            cot_copy.start()
             for r in range(1, n_head):
                 act_copy(r).wait_recv()
-
-        finish_projection(1, chunk)
-        finish_projection(2, chunk)
+            for c in (1, 2):
+                total = partial[c - 1]
+                for r in range(1, n_head):
+                    other = lax.rem(head + n_head - r, n_head)
+                    other = pl.ds(pl.multiple_of(other * features, features), features)
+                    total += dot_nn(acts[:, other], w_vm[0, c, other, :])
+                keep(c, 0, total)
+
+        @pl.when(chunk > 0)
+        def _():
+            project(1, chunk)
+            project(2, chunk)
+
+        pl.when(chunk == chunks - 1)(lambda: weight_copy(0, 0).start())
         for i in range(per):
             h = chunk * per + i
             key_t = qkv[1, h].T
@@ -384,8 +385,9 @@
     cot_copy.wait()
 
     def project_q(chunk, _):
-        own_part(0, chunk)
-        finish_projection(0, chunk)
+        pl.when(chunk + 1 < chunks)(lambda: weight_copy(0, chunk + 1).start())
+        weight_copy(0, chunk).wait()
+        project(0, chunk)
         for i in range(per):
             h = chunk * per + i
             lanes = pl.ds(pl.multiple_of(h * head_dim, head_dim), head_dim)
@@ -525,10 +527,10 @@
         in_specs=[any_spec, any_spec, vmem_spec, any_spec],
         out_specs=[any_spec] * 4,
         scratch_shapes=[
-            pltpu.VMEM((n_head, block, features), BF16),
+            pltpu.VMEM((block, n_head * features), BF16),
             pltpu.VMEM((chunks, 3, w_proj.shape[1], per * head_dim), BF16),
             pltpu.VMEM((block, width), BF16),
-            pltpu.VMEM((3, block, per * head_dim), F32),
+            pltpu.VMEM((2, block, per * head_dim), F32),
             pltpu.VMEM((heads, padded, block), F32),
             pltpu.VMEM((3, heads) + tall, BF16),
             pltpu.VMEM((heads,) + tall, BF16),

time: 47.7 us -> 47 us (0.985)
  Pallas kernels: 46.9 us -> 46.1 us
    pallas_call x1, Pallas kernels: 43.3 us -> 42.5 us  [on_device(): pl.pallas_call(functools.partial(state_kernel, dims), out_shape=results,...]
where the time goes in v1:
time: 47 us; the launch traced here: 46.7 us
  Pallas kernels  46.1 us (98%)
  between operations  0.64 us (1%)
    pallas_call x1, Pallas kernels, on_device(): pl.pallas_call(functools.partial(state_kernel, dims), out_shape=results,...  42.5 us
    pallas_call x1, Pallas kernels, on_device(): pl.pallas_call(functools.partial(hand_over_kernel, pieces), out_shape=res...  3.58 us

profile of v1, /device:TPU:0, one launch (start us, length us, event | category | flops | bytes accessed | tf_op | source)
XLA Modules:
  0.0 46.7 jit_solution(3379167308913920355)
XLA Ops:
  0.6 42.5 %shard_map.75 = (bf16[512,1024]{1,0:T(8,128)(2,1)}, bf16[512,1024]{1,0:T(8,128)(2,1)}, bf16[512,1024]{1,0:T(8,128)(2,1)}, bf16[512,1024]{1,0:T(8,128)(2,1)}) custom-call(bf16[512,1024]{1,0:T(8,128)(2,1)} %act_ref.1, bf16[3,2048,1024]{2,1,0:T(8,128)(2,1)} %w_ref.1, f32[14,8,512]{2,1,0:T(8,128)} %bitcast.1, bf16[512,1024]{1,0:T(8,128)(2,1)} %cot_ref.1), custom_call_target="tpu_custom_call" | custom-call | tf_op jit(solution)/shard_map/pallas_call | solution.py:524
  43.2 3.6 %shard_map.76 = (bf16[512,1024]{1,0:T(8,128)(2,1)}, bf16[512,1024]{1,0:T(8,128)(2,1)}, bf16[512,1024]{1,0:T(8,128)(2,1)}, bf16[512,1024]{1,0:T(8,128)(2,1)}) custom-call(bf16[512,1024]{1,0:T(8,128)(2,1)} %get-tuple-element.8.refs_0_, bf16[512,1024]{1,0:T(8,128)(2,1)} %get-tuple-element.9.refs_1_, bf16[512,1024]{1,0:T(8,128)(2,1)} %get-tuple-element.10.refs_2_, ...), custom_call_target="tpu_custom_call" | custom-call | tf_op jit(solution)/shard_map/pallas_call | solution.py:569

commit v2 on v1

--- a/solution.py
+++ b/solution.py
@@ -442,12 +442,18 @@
             inner[0, h, here, :] = dk_part[a * tile :]
             inner[1, h, here, :] = dv_part[a * tile :]
 
-    def middle(h, _):
-        attend(h)
-        tick(2 * chunks + h, 2 * chunks, heads_end - 1)
+    def middle(chunk, _):
+        for i in range(per):
+            attend(chunk * per + i)
+
+        def advance(i, _):
+            tick(2 * chunks + chunk * per + i, 2 * chunks, heads_end - 1)
+            return 0
+
+        lax.fori_loop(0, per, advance, 0)
         return 0
 
-    lax.fori_loop(0, heads, middle, 0)
+    lax.fori_loop(0, chunks, middle, 0)
 
     def settle(slot, _):
         tick(slot, heads_end, last_slot)

time: 47 us -> 46.7 us (level)
  no operation moved by 1% of the time
where the time goes in v2:
time: 46.7 us; the launch traced here: 46.4 us
  Pallas kernels  45.8 us (98%)
  between operations  0.64 us (1%)
    pallas_call x1, Pallas kernels, on_device(): pl.pallas_call(functools.partial(state_kernel, dims), out_shape=results,...  42.2 us
    pallas_call x1, Pallas kernels, on_device(): pl.pallas_call(functools.partial(hand_over_kernel, pieces), out_shape=res...  3.58 us

profile of v2, /device:TPU:0, one launch (start us, length us, event | category | flops | bytes accessed | tf_op | source)
XLA Modules:
  0.0 46.4 jit_solution(15335463002851585914)
XLA Ops:
  0.6 42.2 %shard_map.75 = (bf16[512,1024]{1,0:T(8,128)(2,1)}, bf16[512,1024]{1,0:T(8,128)(2,1)}, bf16[512,1024]{1,0:T(8,128)(2,1)}, bf16[512,1024]{1,0:T(8,128)(2,1)}) custom-call(bf16[512,1024]{1,0:T(8,128)(2,1)} %act_ref.1, bf16[3,2048,1024]{2,1,0:T(8,128)(2,1)} %w_ref.1, f32[14,8,512]{2,1,0:T(8,128)} %bitcast.1, bf16[512,1024]{1,0:T(8,128)(2,1)} %cot_ref.1), custom_call_target="tpu_custom_call" | custom-call | tf_op jit(solution)/shard_map/pallas_call | solution.py:530
  42.8 3.6 %shard_map.76 = (bf16[512,1024]{1,0:T(8,128)(2,1)}, bf16[512,1024]{1,0:T(8,128)(2,1)}, bf16[512,1024]{1,0:T(8,128)(2,1)}, bf16[512,1024]{1,0:T(8,128)(2,1)}) custom-call(bf16[512,1024]{1,0:T(8,128)(2,1)} %get-tuple-element.8.refs_0_, bf16[512,1024]{1,0:T(8,128)(2,1)} %get-tuple-element.9.refs_1_, bf16[512,1024]{1,0:T(8,128)(2,1)} %get-tuple-element.10.refs_2_, ...), custom_call_target="tpu_custom_call" | custom-call | tf_op jit(solution)/shard_map/pallas_call | solution.py:575
